TPU v7x, 128 devices: a whole 4x4x4 slice. The times are simulated.
128 devices in a mesh: fsdp: 8 (over x, core), blk: 16 (over z, y).
Axes of the slice: x: 4, y: 4, z: 4, core: 2. Of those that a mesh axis runs over, the one named last changes fastest.
Arguments:
- grad: bfloat16 [48, 512, 8192], P('blk', 'fsdp'), may hold values from -6 to 6
- first_moment: bfloat16 [48, 8192, 512], P('fsdp', 'blk'), may hold values from -4 to 4
- second_moment: bfloat16 [48, 8192, 512], P('fsdp', 'blk'), may hold values from 0.049804688 to 2
- left_basis: bfloat16 [48, 8192, 512], P('fsdp', 'blk'), may hold values from -0.25 to 0.25
- right_basis: bfloat16 [48, 8192, 512], P('fsdp', 'blk'), may hold values from -0.25 to 0.25
- block_owner: int32 [48, 16], replicated, may hold values from 0 to 15, as said below
Outputs:
- update: bfloat16 [48, 512, 8192], P('blk', 'fsdp')
- new_first: bfloat16 [48, 8192, 512], P('fsdp', 'blk')
- new_second: bfloat16 [48, 8192, 512], P('fsdp', 'blk')
- owner_load: float32 [8, 16], P('fsdp', 'blk')
Inputs may be any that keep to these rules, and one draw needn't show every extreme that they name: `block_owner`: within each column group, each owner is named by exactly 6 blocks, and the blocks of that group in the 3 bands of one blk index name each owner either 0 or 1 times.
All inputs are finite; a program needn't handle non-finite values.
Results may differ from a plain program's by a relative error of at most 0.0059.
Values may be sent and summed in bfloat16 or wider, within the bound.
A program may use at most 128 MiB of HBM per device.

v0:
```python
import jax
import jax.numpy as jnp
from jax import lax
from jax.experimental import pallas as pl
from jax.experimental.pallas import tpu as pltpu
from jax.sharding import PartitionSpec as P

beta_one = 0.95
beta_two = 0.95
corr_value = 1.0 - 0.95**10
epsilon = 1e-08

MESH = pl.DeviceIdType.MESH
BS = 512
SLOTS = 6
OWNERS = 16
BANDS = 3 * OWNERS
TILES = SLOTS * OWNERS
HALVES = (pl.ds(0, 256), pl.ds(256, 256))
STRIP = BS // OWNERS

BLK_STEPS = (
    (0, 1), (1, 0), (2, 3), (3, 2), (0, 2), (1, 1), (2, 0), (3, 3),
    (0, 3), (1, 2), (2, 1), (3, 0), (0, 0), (1, 3), (2, 2), (3, 1),
)
ROW_STEPS = (
    (0, 1, 0), (1, 0, 1), (2, 1, 0), (3, 0, 1), (0, 0, 0), (1, 1, 1), (2, 0, 0), (3, 1, 1),
    (0, 1, 1), (1, 0, 0), (2, 1, 1), (3, 0, 0), (0, 0, 1), (1, 1, 0), (2, 0, 1), (3, 1, 0),
)


def find_places(owners, table, group):
    names = owners[...]
    row_of = lax.broadcasted_iota(jnp.int32, names.shape, 0)
    bands = names.shape[1]
    sub = lax.broadcasted_iota(jnp.int32, (bands, bands), 0)
    lane = lax.broadcasted_iota(jnp.int32, (bands, bands), 1)

    def upright(row):
        return jnp.sum(jnp.where(sub == lane, row, 0), axis=1, keepdims=True)

    def count(column, row, earlier):
        return jnp.sum(jnp.where((column == row) & earlier, 1, 0), axis=0, keepdims=True)

    first, second = (
        jnp.sum(jnp.where(row_of == group * 2 + i, names, 0), axis=0, keepdims=True) for i in range(2)
    )
    first_up, second_up = upright(first), upright(second)
    place_one = first + OWNERS * (count(first_up, first, sub < lane) + count(second_up, first, sub < lane))
    place_two = second + OWNERS * (count(first_up, second, sub <= lane) + count(second_up, second, sub < lane))
    table[0:1, 0:bands] = jnp.minimum(place_one, TILES - 1)
    table[1:2, 0:bands] = jnp.minimum(place_two, TILES - 1)
    band = lax.broadcasted_iota(jnp.int32, (bands, 128), 0)
    place = lax.broadcasted_iota(jnp.int32, (bands, 128), 1)
    block = jnp.sum(
        jnp.where(upright(place_one) == place, band * 2, 0) + jnp.where(upright(place_two) == place, band * 2 + 1, 0),
        axis=0,
        keepdims=True,
    )
    table[2:3, :] = jnp.minimum(block, TILES - 1)


def kernel(
    owner_names, grad, first, second, left, right,
    update, new_first, new_second, load_ref,
    owners, table, places,
    rows_here, spread_one, spread_two, picked, blocks, ql, qr, mom, var, out_blocks,
    returned_one, returned_two, repacked,
    turned, rotated, direction, back,
    stage_sem, send_sem, one_sem, block_sem, state_sem,
):
    f = lax.axis_index("fsdp")
    b = lax.axis_index("blk")
    x, c, z, y = f // 2, f % 2, b // 4, b % 4

    def row_target(step):
        dz, parity, bit = step
        tz, half, gc = (z + dz + 2 * c) % 4, (y + parity) % 2, (y // 2 + bit) % 2
        gx = (x - tz - 2 * gc + 8) % 4
        return gx * 2 + gc, tz * 4 + 2 * c + half, half

    def blk_target(step):
        dz, dy = step
        return (z + dz + 2 * c) % 4 * 4 + (y + dy + 2 * c) % 4

    def strip_rows(middle):
        strip = ((x + 2 * c + middle // 4) % 4) * 4 + middle % 4
        return pl.ds(pl.multiple_of(strip * STRIP, STRIP), STRIP)

    home = ((x + z + 2 * c) % 4) * 2 + y // 2
    home_half = y % 2
    mine = home == f

    def unless_here(tf, tb, send, keep, always):
        if always:
            send()
            return
        here = (tf == f) & (tb == b)
        pl.when(jnp.logical_not(here))(send)
        if keep is not None:
            pl.when(here)(keep)

    def pass_on(source, place, sent, arrived, tf, tb, always):
        def send():
            pltpu.make_async_remote_copy(
                source, place, sent, arrived, device_id=(tf, tb), device_id_type=MESH
            ).start()

        def keep():
            pltpu.make_async_copy(source, place, arrived).start()

        unless_here(tf, tb, send, keep, always)

    spread = (spread_one, spread_two)
    returned = (returned_one, returned_two)
    staging = pltpu.make_async_copy(grad, rows_here, stage_sem.at[0])
    staging.start()
    barrier = pltpu.get_barrier_semaphore()

    def greet(tf, tb, always):
        def send():
            pl.semaphore_signal(barrier, inc=1, device_id=(tf, tb), device_id_type=MESH)

        unless_here(tf, tb, send, None, always)

    for step in BLK_STEPS:
        greet(f, blk_target(step), step not in ((0, 0), (2, 2)))
        greet(home, blk_target(step), step not in ((0, 0), (2, 2)))
    for step in ROW_STEPS:
        tf, tb, _ = row_target(step)
        greet(tf, tb, step[0] % 2 == 1)
    pl.semaphore_wait(barrier, 47 - 2 * mine.astype(jnp.int32))

    staging.wait()
    for part in range(2):

        @pl.loop(0, SLOTS)
        def _(p):
            for step in ROW_STEPS:
                tf, tb, half = row_target(step)
                source = rows_here.at[
                    p // 2,
                    pl.ds(pl.multiple_of(half * STRIP, STRIP), STRIP),
                    pl.ds(pl.multiple_of(tf * (2 * BS) + p % 2 * BS + part * 256, 256), 256),
                ]
                pass_on(
                    source, spread[part].at[b * SLOTS + p],
                    send_sem.at[0], one_sem.at[4 * part], tf, tb, step[0] % 2 == 1,
                )

    states = [
        pltpu.make_async_copy(array, held, state_sem.at[i])
        for i, (array, held) in enumerate(((left, ql), (right, qr), (first, mom), (second, var)))
    ]
    copy = pltpu.make_async_copy(owner_names, owners, state_sem.at[4])
    copy.start()
    for state in states:
        state.start()
    copy.wait()
    find_places(owners, table, f)
    copy = pltpu.make_async_copy(table, places, state_sem.at[4])
    copy.start()
    copy.wait()
    rows = strip_rows(b)
    for half, columns in enumerate(HALVES):
        pltpu.make_async_copy(spread[half], spread[half], one_sem.at[4 * half]).wait()

        @pl.loop(0, SLOTS)
        def _(s):
            @pl.loop(0, OWNERS)
            def _(o):
                picked[s * OWNERS + o, :, columns] = spread[half][places[2, s * OWNERS + o]]

            for step in BLK_STEPS:
                target = blk_target(step)
                pass_on(
                    picked.at[s * OWNERS + target, :, columns], blocks.at[s, rows, columns],
                    send_sem.at[1], block_sem.at[s] if half else one_sem.at[5],
                    f, target, step not in ((0, 0), (2, 2)),
                )

    part = blocks.at[:, :, HALVES[0]]
    pltpu.make_async_copy(part, part, one_sem.at[5]).wait()
    for state in states:
        state.wait()

    def block_step(s, total):
        part = blocks.at[s, :, HALVES[1]]
        pltpu.make_async_copy(part, part, block_sem.at[s]).wait()
        turned[...] = lax.dot_general(
            ql[s], blocks[s], (((0,), (0,)), ((), ())), preferred_element_type=jnp.float32
        ).astype(jnp.bfloat16)
        rotated[...] = jnp.dot(turned[...], qr[s], preferred_element_type=jnp.float32)

        @pl.loop(0, BS // 16)
        def _(i):
            rows = pl.ds(pl.multiple_of(i * 16, 16), 16)
            turn = rotated[rows]
            first_next = beta_one * mom[s, rows].astype(jnp.float32) + (1.0 - beta_one) * turn
            second_next = beta_two * var[s, rows].astype(jnp.float32) + (1.0 - beta_two) * turn * turn
            new_first[s, rows] = first_next.astype(jnp.bfloat16)
            new_second[s, rows] = second_next.astype(jnp.bfloat16)
            direction[rows] = (
                first_next / corr_value / (jnp.sqrt(second_next / corr_value) + epsilon)
            ).astype(jnp.bfloat16)

        back[...] = jnp.dot(ql[s], direction[...], preferred_element_type=jnp.float32).astype(jnp.bfloat16)
        for half in range(2):
            rows = pl.ds(half * 256, 256)
            done = lax.dot_general(
                back[rows], qr[s], (((1,), (1,)), ((), ())), preferred_element_type=jnp.float32
            )
            out_blocks[s, rows] = done.astype(jnp.bfloat16)
            total = total + jnp.sum((done * done).reshape(32, 8, BS), axis=0)
        for step in BLK_STEPS:
            target = blk_target(step)
            pass_on(
                out_blocks.at[s, strip_rows(target), HALVES[0]], returned[0].at[s * OWNERS + b],
                send_sem.at[2], one_sem.at[1],
                f, target, step not in ((0, 0), (2, 2)),
            )
        return total

    total = lax.fori_loop(0, SLOTS, block_step, jnp.zeros((8, BS), jnp.float32))
    load_ref[0, 0] = jnp.sum(total) / (BS * BS)

    @pl.loop(0, SLOTS)
    def _(s):
        for step in BLK_STEPS:
            target = blk_target(step)
            pass_on(
                out_blocks.at[s, strip_rows(target), HALVES[1]], returned[1].at[s * OWNERS + b],
                send_sem.at[2], one_sem.at[3],
                f, target, step not in ((0, 0), (2, 2)),
            )

    for half, columns in enumerate(HALVES):
        pltpu.make_async_copy(returned[half], returned[half], one_sem.at[1 + 2 * half]).wait()

        @pl.loop(0, SLOTS)
        def _(p):
            @pl.loop(0, OWNERS)
            def _(t):
                repacked[t * SLOTS + p, :, columns] = returned[half][places[p % 2, t * 3 + p // 2]]

            place = update.at[
                p // 2,
                pl.ds(pl.multiple_of(home_half * STRIP, STRIP), STRIP),
                pl.ds(pl.multiple_of(f * (2 * BS) + p % 2 * BS + half * 256, 256), 256),
            ]
            for step in BLK_STEPS:
                target = blk_target(step)
                pass_on(
                    repacked.at[target * SLOTS + p, :, columns],
                    place, send_sem.at[3], one_sem.at[2],
                    home, target, step not in ((0, 0), (2, 2)),
                )

    few = blocks.at[:, pl.ds(0, BS - STRIP)]
    for i in (1, 2):
        pltpu.make_async_copy(few, few, send_sem.at[i]).wait()

    @pl.when(mine)
    def _():
        for i in (0, 3):
            pltpu.make_async_copy(few, few, send_sem.at[i]).wait()

    @pl.when(jnp.logical_not(mine))
    def _():
        for i in (0, 3):
            pltpu.make_async_copy(blocks, blocks, send_sem.at[i]).wait()

    pltpu.make_async_copy(update, update, one_sem.at[2]).wait()


def write_out(*refs):
    count = (len(refs) - 1) // 2
    parts = []
    for i, (held, out) in enumerate(zip(refs[:count], refs[count:-1])):
        size = held.shape[0] // 3
        for k in range(3):
            rows = pl.ds(k * size, size)
            parts.append(pltpu.make_async_copy(held.at[rows], out.at[rows], refs[-1].at[i * 3 + k]))
    for part in parts:
        part.start()
    for part in parts:
        part.wait()


def body(grad, first_moment, second_moment, left_basis, right_basis, block_owner):
    bf = jnp.bfloat16
    state = pltpu.VMEM(first_moment.shape, bf)
    kept = pl.BlockSpec(memory_space=pltpu.VMEM)
    whole = pl.BlockSpec(memory_space=pl.ANY)
    scalar = pl.BlockSpec(memory_space=pltpu.SMEM)
    strips = pltpu.VMEM((TILES, STRIP, BS), bf)
    halves = pltpu.VMEM((TILES, STRIP, BS // 2), bf)
    held = pltpu.VMEM((SLOTS, BS, BS), bf)
    one = pltpu.VMEM((BS, BS), bf)
    *results, load = pl.pallas_call(
        kernel,
        out_shape=(
            pltpu.VMEM(grad.shape, bf),
            state,
            state,
            jax.ShapeDtypeStruct((1, 1), jnp.float32),
        ),
        in_specs=[whole] * 6,
        out_specs=(kept, kept, kept, scalar),
        scratch_shapes=[
            pltpu.VMEM((OWNERS, BANDS), jnp.int32),
            pltpu.VMEM((8, 128), jnp.int32),
            pltpu.SMEM((8, 128), jnp.int32),
            pltpu.VMEM(grad.shape, bf), halves, halves, strips, held, held, held, held, held, held,
            halves, halves, strips,
            one, pltpu.VMEM((BS, BS), jnp.float32), one, one,
            pltpu.SemaphoreType.DMA((1,)),
            pltpu.SemaphoreType.DMA((4,)),
            pltpu.SemaphoreType.DMA((6,)),
            pltpu.SemaphoreType.DMA((SLOTS,)),
            pltpu.SemaphoreType.DMA((5,)),
        ],
        compiler_params=pltpu.CompilerParams(
            collective_id=0, has_side_effects=True, vmem_limit_bytes=52 * 1024 * 1024
        ),
    )(block_owner.T, grad, first_moment, second_moment, left_basis, right_basis)
    outs = [jax.ShapeDtypeStruct(r.shape, r.dtype) for r in results]
    written = pl.pallas_call(
        write_out,
        out_shape=outs,
        in_specs=[whole] * len(outs),
        out_specs=[whole] * len(outs),
        scratch_shapes=[pltpu.SemaphoreType.DMA((3 * len(outs),))],
        compiler_params=pltpu.CompilerParams(vmem_limit_bytes=1024 * 1024),
    )(*results)
    return (*written, load)


def solution(mesh):
    placed = (
        P("blk", "fsdp", None),
        P("fsdp", "blk", None),
        P("fsdp", "blk", None),
        P("fsdp", "blk", None),
        P("fsdp", "blk", None),
        P(),
    )
    return jax.shard_map(
        body,
        mesh=mesh,
        in_specs=placed,
        out_specs=(
            P("blk", "fsdp", None),
            P("fsdp", "blk", None),
            P("fsdp", "blk", None),
            P("fsdp", "blk"),
        ),
        check_vma=False,
    )
```

profile of v0, /device:TPU:1, one launch (start us, length us, event | category | flops | bytes accessed | tf_op | source)
XLA Modules:
  0.0 159.9 jit_solution(8341123980750863786)
XLA Ops:
  0.6 153.8 %shard_map.93 = (bf16[3,64,8192]{2,1,0:T(8,128)(2,1)S(1)}, bf16[6,512,512]{2,1,0:T(8,128)(2,1)S(1)}, bf16[6,512,512]{2,1,0:T(8,128)(2,1)S(1)}, f32[1,1]{1,0:T(1,128)}) custom-call(s32[16,48]{1,0:T(8,128)} %bitcast.1, bf16[3,64,8192]{2,1,0:T(8,128)(2,1)} %grad.1, bf16[6,512,512]{2,1,0:T(8,128)(2,1)} %first.1, bf16[6,512,512]{2,1,0:T(8,128)(2,1)} %second.1, ...), custom_call_target="tpu_custom_call" | custom-call | tf_op jit(solution)/shard_map/pallas_call | solution.py:300
  154.4 3.7 %shard_map.94 = (bf16[3,64,8192]{2,1,0:T(8,128)(2,1)}, bf16[6,512,512]{2,1,0:T(8,128)(2,1)}, bf16[6,512,512]{2,1,0:T(8,128)(2,1)}) custom-call(bf16[3,64,8192]{2,1,0:T(8,128)(2,1)S(1)} %get-tuple-element.11.refs_0_, bf16[6,512,512]{2,1,0:T(8,128)(2,1)S(1)} %get-tuple-element.12.refs_1_, bf16[6,512,512]{2,1,0:T(8,128)(2,1)S(1)} %get-tuple-element.13.refs_2_), custom_call_target="tpu_custom_call" | custom-call | tf_op jit(solution)/shard_map/pallas_call | solution.py:328
where the time goes:
time: 160 us
  Pallas kernels  157 us (98%)
  between operations  2.41 us (2%)
    pallas_call x1, Pallas kernels, body(): pl.pallas_call(kernel, out_shape=(pltpu.VMEM(grad.shape, bf), state, stat...  154 us
    pallas_call x1, Pallas kernels, body(): pl.pallas_call(write_out, out_shape=outs, in_specs=[whole] * len(outs), o...  3.69 us

commit v1 on v0

--- a/solution.py
+++ b/solution.py
@@ -91,6 +91,9 @@
     home_half = y % 2
     mine = home == f
 
+    row_targets = [row_target(step) for step in ROW_STEPS]
+    blk_targets = [blk_target(step) for step in BLK_STEPS]
+
     def unless_here(tf, tb, send, keep, always):
         if always:
             send()
@@ -123,11 +126,10 @@
 
         unless_here(tf, tb, send, None, always)
 
-    for step in BLK_STEPS:
-        greet(f, blk_target(step), step not in ((0, 0), (2, 2)))
-        greet(home, blk_target(step), step not in ((0, 0), (2, 2)))
-    for step in ROW_STEPS:
-        tf, tb, _ = row_target(step)
+    for step, target in zip(BLK_STEPS, blk_targets):
+        greet(f, target, step not in ((0, 0), (2, 2)))
+        greet(home, target, step not in ((0, 0), (2, 2)))
+    for step, (tf, tb, _) in zip(ROW_STEPS, row_targets):
         greet(tf, tb, step[0] % 2 == 1)
     pl.semaphore_wait(barrier, 47 - 2 * mine.astype(jnp.int32))
 
@@ -136,8 +138,7 @@
 
         @pl.loop(0, SLOTS)
         def _(p):
-            for step in ROW_STEPS:
-                tf, tb, half = row_target(step)
+            for step, (tf, tb, half) in zip(ROW_STEPS, row_targets):
                 source = rows_here.at[
                     p // 2,
                     pl.ds(pl.multiple_of(half * STRIP, STRIP), STRIP),
@@ -171,8 +172,7 @@
             def _(o):
                 picked[s * OWNERS + o, :, columns] = spread[half][places[2, s * OWNERS + o]]
 
-            for step in BLK_STEPS:
-                target = blk_target(step)
+            for step, target in zip(BLK_STEPS, blk_targets):
                 pass_on(
                     picked.at[s * OWNERS + target, :, columns], blocks.at[s, rows, columns],
                     send_sem.at[1], block_sem.at[s] if half else one_sem.at[5],
@@ -212,8 +212,7 @@
             )
             out_blocks[s, rows] = done.astype(jnp.bfloat16)
             total = total + jnp.sum((done * done).reshape(32, 8, BS), axis=0)
-        for step in BLK_STEPS:
-            target = blk_target(step)
+        for step, target in zip(BLK_STEPS, blk_targets):
             pass_on(
                 out_blocks.at[s, strip_rows(target), HALVES[0]], returned[0].at[s * OWNERS + b],
                 send_sem.at[2], one_sem.at[1],
@@ -226,8 +225,7 @@
 
     @pl.loop(0, SLOTS)
     def _(s):
-        for step in BLK_STEPS:
-            target = blk_target(step)
+        for step, target in zip(BLK_STEPS, blk_targets):
             pass_on(
                 out_blocks.at[s, strip_rows(target), HALVES[1]], returned[1].at[s * OWNERS + b],
                 send_sem.at[2], one_sem.at[3],
@@ -248,8 +246,7 @@
                 pl.ds(pl.multiple_of(home_half * STRIP, STRIP), STRIP),
                 pl.ds(pl.multiple_of(f * (2 * BS) + p % 2 * BS + half * 256, 256), 256),
             ]
-            for step in BLK_STEPS:
-                target = blk_target(step)
+            for step, target in zip(BLK_STEPS, blk_targets):
                 pass_on(
                     repacked.at[target * SLOTS + p, :, columns],
                     place, send_sem.at[3], one_sem.at[2],

time: 160 us -> 160 us (level)
  no operation moved by 1% of the time
where the time goes in v1:
time: 160 us
  Pallas kernels  158 us (99%)
  between operations  2.41 us (2%)
    pallas_call x1, Pallas kernels, body(): pl.pallas_call(kernel, out_shape=(pltpu.VMEM(grad.shape, bf), state, stat...  154 us
    pallas_call x1, Pallas kernels, body(): pl.pallas_call(write_out, out_shape=outs, in_specs=[whole] * len(outs), o...  3.69 us

profile of v1, /device:TPU:1, one launch (start us, length us, event | category | flops | bytes accessed | tf_op | source)
XLA Modules:
  0.0 159.9 jit_solution(16159849121798528694)
XLA Ops:
  0.6 153.8 %shard_map.93 = (bf16[3,64,8192]{2,1,0:T(8,128)(2,1)S(1)}, bf16[6,512,512]{2,1,0:T(8,128)(2,1)S(1)}, bf16[6,512,512]{2,1,0:T(8,128)(2,1)S(1)}, f32[1,1]{1,0:T(1,128)}) custom-call(s32[16,48]{1,0:T(8,128)} %bitcast.1, bf16[3,64,8192]{2,1,0:T(8,128)(2,1)} %grad.1, bf16[6,512,512]{2,1,0:T(8,128)(2,1)} %first.1, bf16[6,512,512]{2,1,0:T(8,128)(2,1)} %second.1, ...), custom_call_target="tpu_custom_call" | custom-call | tf_op jit(solution)/shard_map/pallas_call | solution.py:297
  154.5 3.7 %shard_map.94 = (bf16[3,64,8192]{2,1,0:T(8,128)(2,1)}, bf16[6,512,512]{2,1,0:T(8,128)(2,1)}, bf16[6,512,512]{2,1,0:T(8,128)(2,1)}) custom-call(bf16[3,64,8192]{2,1,0:T(8,128)(2,1)S(1)} %get-tuple-element.11.refs_0_, bf16[6,512,512]{2,1,0:T(8,128)(2,1)S(1)} %get-tuple-element.12.refs_1_, bf16[6,512,512]{2,1,0:T(8,128)(2,1)S(1)} %get-tuple-element.13.refs_2_), custom_call_target="tpu_custom_call" | custom-call | tf_op jit(solution)/shard_map/pallas_call | solution.py:325

commit v2 on v1

--- a/solution.py
+++ b/solution.py
@@ -184,6 +184,14 @@
     for state in states:
         state.wait()
 
+    def late(s):
+        for step, target in zip(BLK_STEPS, blk_targets):
+            pass_on(
+                out_blocks.at[s, strip_rows(target), HALVES[1]], returned[1].at[s * OWNERS + b],
+                send_sem.at[2], one_sem.at[3],
+                f, target, step not in ((0, 0), (2, 2)),
+            )
+
     def block_step(s, total):
         part = blocks.at[s, :, HALVES[1]]
         pltpu.make_async_copy(part, part, block_sem.at[s]).wait()
@@ -218,19 +226,16 @@
                 send_sem.at[2], one_sem.at[1],
                 f, target, step not in ((0, 0), (2, 2)),
             )
+        @pl.when(s >= 3)
+        def _():
+            late(s - 3)
+
         return total
 
     total = lax.fori_loop(0, SLOTS, block_step, jnp.zeros((8, BS), jnp.float32))
     load_ref[0, 0] = jnp.sum(total) / (BS * BS)
 
-    @pl.loop(0, SLOTS)
-    def _(s):
-        for step, target in zip(BLK_STEPS, blk_targets):
-            pass_on(
-                out_blocks.at[s, strip_rows(target), HALVES[1]], returned[1].at[s * OWNERS + b],
-                send_sem.at[2], one_sem.at[3],
-                f, target, step not in ((0, 0), (2, 2)),
-            )
+    pl.loop(3, SLOTS)(late)
 
     for half, columns in enumerate(HALVES):
         pltpu.make_async_copy(returned[half], returned[half], one_sem.at[1 + 2 * half]).wait()

time: 160 us -> 160 us (level)
  no operation moved by 1% of the time
where the time goes in v2:
time: 160 us
  Pallas kernels  158 us (99%)
  between operations  2.41 us (2%)
    pallas_call x1, Pallas kernels, body(): pl.pallas_call(kernel, out_shape=(pltpu.VMEM(grad.shape, bf), state, stat...  154 us
    pallas_call x1, Pallas kernels, body(): pl.pallas_call(write_out, out_shape=outs, in_specs=[whole] * len(outs), o...  3.69 us

profile of v2, /device:TPU:1, one launch (start us, length us, event | category | flops | bytes accessed | tf_op | source)
XLA Modules:
  0.0 159.9 jit_solution(10148903133039539884)
XLA Ops:
  0.6 153.8 %shard_map.93 = (bf16[3,64,8192]{2,1,0:T(8,128)(2,1)S(1)}, bf16[6,512,512]{2,1,0:T(8,128)(2,1)S(1)}, bf16[6,512,512]{2,1,0:T(8,128)(2,1)S(1)}, f32[1,1]{1,0:T(1,128)}) custom-call(s32[16,48]{1,0:T(8,128)} %bitcast.1, bf16[3,64,8192]{2,1,0:T(8,128)(2,1)} %grad.1, bf16[6,512,512]{2,1,0:T(8,128)(2,1)} %first.1, bf16[6,512,512]{2,1,0:T(8,128)(2,1)} %second.1, ...), custom_call_target="tpu_custom_call" | custom-call | tf_op jit(solution)/shard_map/pallas_call | solution.py:302
  154.5 3.7 %shard_map.94 = (bf16[3,64,8192]{2,1,0:T(8,128)(2,1)}, bf16[6,512,512]{2,1,0:T(8,128)(2,1)}, bf16[6,512,512]{2,1,0:T(8,128)(2,1)}) custom-call(bf16[3,64,8192]{2,1,0:T(8,128)(2,1)S(1)} %get-tuple-element.11.refs_0_, bf16[6,512,512]{2,1,0:T(8,128)(2,1)S(1)} %get-tuple-element.12.refs_1_, bf16[6,512,512]{2,1,0:T(8,128)(2,1)S(1)} %get-tuple-element.13.refs_2_), custom_call_target="tpu_custom_call" | custom-call | tf_op jit(solution)/shard_map/pallas_call | solution.py:330

commit v3 on v0

--- a/solution.py
+++ b/solution.py
@@ -126,10 +126,7 @@
     for step in BLK_STEPS:
         greet(f, blk_target(step), step not in ((0, 0), (2, 2)))
         greet(home, blk_target(step), step not in ((0, 0), (2, 2)))
-    for step in ROW_STEPS:
-        tf, tb, _ = row_target(step)
-        greet(tf, tb, step[0] % 2 == 1)
-    pl.semaphore_wait(barrier, 47 - 2 * mine.astype(jnp.int32))
+    pl.semaphore_wait(barrier, 31 - mine.astype(jnp.int32))
 
     staging.wait()
     for part in range(2):

time: 160 us -> 159 us (level)
  no operation moved by 1% of the time
where the time goes in v3:
time: 159 us
  Pallas kernels  157 us (99%)
  between operations  2.41 us (2%)
    pallas_call x1, Pallas kernels, body(): pl.pallas_call(kernel, out_shape=(pltpu.VMEM(grad.shape, bf), state, stat...  153 us
    pallas_call x1, Pallas kernels, body(): pl.pallas_call(write_out, out_shape=outs, in_specs=[whole] * len(outs), o...  3.69 us

profile of v3, /device:TPU:1, one launch (start us, length us, event | category | flops | bytes accessed | tf_op | source)
XLA Modules:
  0.0 159.3 jit_solution(6009105332816619659)
XLA Ops:
  0.6 153.2 %shard_map.93 = (bf16[3,64,8192]{2,1,0:T(8,128)(2,1)S(1)}, bf16[6,512,512]{2,1,0:T(8,128)(2,1)S(1)}, bf16[6,512,512]{2,1,0:T(8,128)(2,1)S(1)}, f32[1,1]{1,0:T(1,128)}) custom-call(s32[16,48]{1,0:T(8,128)} %bitcast.1, bf16[3,64,8192]{2,1,0:T(8,128)(2,1)} %grad.1, bf16[6,512,512]{2,1,0:T(8,128)(2,1)} %first.1, bf16[6,512,512]{2,1,0:T(8,128)(2,1)} %second.1, ...), custom_call_target="tpu_custom_call" | custom-call | tf_op jit(solution)/shard_map/pallas_call | solution.py:297
  153.8 3.7 %shard_map.94 = (bf16[3,64,8192]{2,1,0:T(8,128)(2,1)}, bf16[6,512,512]{2,1,0:T(8,128)(2,1)}, bf16[6,512,512]{2,1,0:T(8,128)(2,1)}) custom-call(bf16[3,64,8192]{2,1,0:T(8,128)(2,1)S(1)} %get-tuple-element.11.refs_0_, bf16[6,512,512]{2,1,0:T(8,128)(2,1)S(1)} %get-tuple-element.12.refs_1_, bf16[6,512,512]{2,1,0:T(8,128)(2,1)S(1)} %get-tuple-element.13.refs_2_), custom_call_target="tpu_custom_call" | custom-call | tf_op jit(solution)/shard_map/pallas_call | solution.py:325

commit v4 on v3

--- a/solution.py
+++ b/solution.py
@@ -115,6 +115,12 @@
     returned = (returned_one, returned_two)
     staging = pltpu.make_async_copy(grad, rows_here, stage_sem.at[0])
     staging.start()
+    states = [
+        pltpu.make_async_copy(array, held, state_sem.at[i])
+        for i, (array, held) in enumerate(((left, ql), (right, qr), (first, mom), (second, var)))
+    ]
+    for state in states:
+        state.start()
     barrier = pltpu.get_barrier_semaphore()
 
     def greet(tf, tb, always):
@@ -145,14 +151,8 @@
                     send_sem.at[0], one_sem.at[4 * part], tf, tb, step[0] % 2 == 1,
                 )
 
-    states = [
-        pltpu.make_async_copy(array, held, state_sem.at[i])
-        for i, (array, held) in enumerate(((left, ql), (right, qr), (first, mom), (second, var)))
-    ]
     copy = pltpu.make_async_copy(owner_names, owners, state_sem.at[4])
     copy.start()
-    for state in states:
-        state.start()
     copy.wait()
     find_places(owners, table, f)
     copy = pltpu.make_async_copy(table, places, state_sem.at[4])

time: 159 us -> 162 us (1.019); the launches traced: 159 us -> 160 us
  no operation moved by 1% of the time
where the time goes in v4:
time: 162 us; the launch traced here: 160 us
  Pallas kernels  157 us (97%)
  between operations  2.41 us (1%)
    pallas_call x1, Pallas kernels, body(): pl.pallas_call(kernel, out_shape=(pltpu.VMEM(grad.shape, bf), state, stat...  154 us
    pallas_call x1, Pallas kernels, body(): pl.pallas_call(write_out, out_shape=outs, in_specs=[whole] * len(outs), o...  3.69 us

profile of v4, /device:TPU:1, one launch (start us, length us, event | category | flops | bytes accessed | tf_op | source)
XLA Modules:
  0.0 159.9 jit_solution(13361570747111974789)
XLA Ops:
  0.6 153.8 %shard_map.93 = (bf16[3,64,8192]{2,1,0:T(8,128)(2,1)S(1)}, bf16[6,512,512]{2,1,0:T(8,128)(2,1)S(1)}, bf16[6,512,512]{2,1,0:T(8,128)(2,1)S(1)}, f32[1,1]{1,0:T(1,128)}) custom-call(s32[16,48]{1,0:T(8,128)} %bitcast.1, bf16[3,64,8192]{2,1,0:T(8,128)(2,1)} %grad.1, bf16[6,512,512]{2,1,0:T(8,128)(2,1)} %first.1, bf16[6,512,512]{2,1,0:T(8,128)(2,1)} %second.1, ...), custom_call_target="tpu_custom_call" | custom-call | tf_op jit(solution)/shard_map/pallas_call | solution.py:297
  154.4 3.7 %shard_map.94 = (bf16[3,64,8192]{2,1,0:T(8,128)(2,1)}, bf16[6,512,512]{2,1,0:T(8,128)(2,1)}, bf16[6,512,512]{2,1,0:T(8,128)(2,1)}) custom-call(bf16[3,64,8192]{2,1,0:T(8,128)(2,1)S(1)} %get-tuple-element.11.refs_0_, bf16[6,512,512]{2,1,0:T(8,128)(2,1)S(1)} %get-tuple-element.12.refs_1_, bf16[6,512,512]{2,1,0:T(8,128)(2,1)S(1)} %get-tuple-element.13.refs_2_), custom_call_target="tpu_custom_call" | custom-call | tf_op jit(solution)/shard_map/pallas_call | solution.py:325
